TPU v7x, 128 devices: a whole 4x4x4 slice. The times are simulated.
128 devices in a mesh: blk: 16 (over z, y), owner: 8 (over x, core).
Axes of the slice: x: 4, y: 4, z: 4, core: 2. Of those that a mesh axis runs over, the one named last changes fastest.
Arguments:
- small_emb: bfloat16 [16384, 4096], P(('blk', 'owner'))
- cluster_of: int32 [16384], P(('blk', 'owner')), may hold values from 0 to 2047, as said below
- big_emb: bfloat16 [32768, 4096], P(('blk', 'owner'))
Outputs:
- small_max: float32 [16384], P(('blk', 'owner'))
- big_max: float32 [32768], P(('blk', 'owner'))
Inputs may be any that keep to these rules, and one draw needn't show every extreme that they name: `cluster_of`: cluster c is owned by device c // 16 of the joined axes blk+owner. At most 2 documents of one device lie in the clusters of one owner; in every draw one owner receives exactly 2 documents from every device.
All inputs are finite; a program needn't handle non-finite values.
Results may differ from a plain program's by a relative error of at most 0.00045.
Values may be sent and summed in bfloat16 or wider, within the bound.
A program may use at most 128 MiB of HBM per device.

v0:
```python
import jax
import jax.numpy as jnp
from jax import lax
from jax.sharding import PartitionSpec as P

CPO = 16


def unit_rows(matrix):
    values = matrix.astype(jnp.float32)
    inverse = lax.rsqrt(jnp.sum(values * values, axis=-1, keepdims=True) + 1e-06)
    return (values * inverse).astype(jnp.bfloat16)


def inner_block(left_rows, right_rows):
    return lax.dot_general(
        left_rows, right_rows, (((1,), (1,)), ((), ())), preferred_element_type=jnp.float32
    )


def body(small_emb, cluster_of, big_emb):
    devices = lax.axis_size(("blk", "owner"))
    row_count, width = small_emb.shape
    capacity = 2 * row_count // devices
    small_units = unit_rows(small_emb)
    target_owner = cluster_of // CPO
    row_ids = jnp.arange(row_count, dtype=jnp.int32)
    same_owner = target_owner[:, None] == target_owner[None, :]
    earlier = row_ids[None, :] < row_ids[:, None]
    slot_rank = jnp.sum((same_owner & earlier).astype(jnp.int32), axis=1)
    flat_slot = target_owner * capacity + slot_rank
    outgoing = jnp.zeros((devices * capacity, width), jnp.bfloat16).at[flat_slot].set(small_units)
    out_labels = jnp.full((devices * capacity,), -1, jnp.int32).at[flat_slot].set(cluster_of)
    arrived, in_labels = (
        lax.all_to_all(
            outgoing.reshape(devices, capacity, width),
            ("blk", "owner"),
            split_axis=0,
            concat_axis=0,
            tiled=True,
        ),
        lax.all_to_all(
            out_labels.reshape(devices, capacity),
            ("blk", "owner"),
            split_axis=0,
            concat_axis=0,
            tiled=True,
        ),
    )
    arrived = arrived.reshape(devices * capacity, width)
    in_labels = in_labels.reshape(devices * capacity)
    slot_ids = jnp.arange(devices * capacity, dtype=jnp.int32)
    gram = inner_block(arrived, arrived)
    keep = (
        (in_labels[:, None] == in_labels[None, :])
        & (slot_ids[:, None] != slot_ids[None, :])
        & (in_labels[None, :] >= 0)
    )
    owner_best = jnp.max(jnp.where(keep, gram, jnp.float32(-1.0)), axis=1)
    returned = lax.all_to_all(
        owner_best.reshape(devices, capacity),
        ("blk", "owner"),
        split_axis=0,
        concat_axis=0,
        tiled=True,
    )
    small_max = returned.reshape(-1)[flat_slot]
    big_units = unit_rows(big_emb)
    big_count = big_units.shape[0]
    my_block = lax.axis_index("blk")
    big_ids = jnp.arange(big_count, dtype=jnp.int32)
    global_rows = my_block * big_count + big_ids
    piece = lax.all_gather(big_units, "blk", axis=0, tiled=True)
    scores = inner_block(big_units, piece)
    global_cols = jnp.arange(piece.shape[0], dtype=jnp.int32)
    scores = jnp.where(global_rows[:, None] == global_cols[None, :], jnp.float32(-1.0), scores)
    big_max = jnp.maximum(jnp.full((big_count,), -1.0, jnp.float32), jnp.max(scores, axis=1))
    return (small_max, big_max)


def solution(mesh):
    return jax.shard_map(
        body,
        mesh=mesh,
        in_specs=(P(("blk", "owner"), None), P(("blk", "owner")), P(("blk", "owner"), None)),
        out_specs=(P(("blk", "owner")), P(("blk", "owner"))),
        check_vma=False,
    )
```

profile of v0, /device:TPU:1, one launch (start us, length us, event | category | flops | bytes accessed | tf_op | source)
XLA Modules:
  0.0 256.6 jit_solution(7068237138198947149)
XLA Ops:
  7.2 0.0 copy-start
  7.2 0.0 all-gather.2.cloned.1.call-start
  7.2 2.2 fusion
  9.5 0.0 copy-done
  9.5 1.9 fusion.1
  11.4 0.0 copy-start.3
  11.4 0.0 copy-start.2
  11.4 0.0 all-gather.2.cloned.1.call-update
  11.4 0.6 copy-done.3
  12.0 0.2 convert_reduce_fusion
  12.2 1.0 scatter_custom_fusion
  13.2 0.8 all_to_all.15
  14.0 11.5 %all-to-all-start = ((s32[128,1,2]{2,1,0:T(1,128)}), s32[128,1,2]{2,1,0:T(1,128)S(1)}, u32[]{:S(2)}, u32[]{:S(2)}) async-start(s32[128,1,2]{2,1,0:T(1,128)} %bitcast), calls=%async_computation | async-start | bytes 131072 | tf_op jit(solution)/shard_map/all_to_all | solution.py:42
  25.5 0.0 copy-done.2
  25.5 0.3 fusion.2
  25.8 2.8 %scatter_custom_fusion.1 = bf16[256,4096]{1,0:T(8,128)(2,1)S(1)} fusion(s32[128]{0:T(128)S(1)} %compare_select_fusion, bf16[128,4096]{1,0:T(8,128)(2,1)S(1)} %copy-done.2, f32[128]{0:T(128)S(1)} %add_rsqrt_fusion.1, bf16[]{:T(256)} %constant.12.clone.1), kind=kCustom, calls=%fused_computation.16 | custom fusion | flops 1572864 | bytes 3146242 | tf_op jit(solution)/shard_map/scatter | solution.py:32
  28.6 2.7 %reshape.52 = bf16[128,2,4096]{2,1,0:T(2,128)(2,1)} reshape(bf16[256,4096]{1,0:T(8,128)(2,1)S(1)} %scatter_custom_fusion.1) | data formatting | bytes 4194304 | tf_op jit(solution)/shard_map/reshape | solution.py:36
  31.3 3.8 %all-to-all-done = s32[128,1,2]{2,1,0:T(1,128)S(1)} async-done(((s32[128,1,2]{2,1,0:T(1,128)}), s32[128,1,2]{2,1,0:T(1,128)S(1)}, u32[]{:S(2)}, u32[]{:S(2)}) %all-to-all-start) | async-done | bytes 1056 | tf_op jit(solution)/shard_map/all_to_all | solution.py:42
  35.1 5.9 %all-to-all-start.1 = ((bf16[128,2,4096]{2,1,0:T(2,128)(2,1)}), bf16[128,2,4096]{2,1,0:T(2,128)(2,1)S(1)}, u32[]{:S(2)}, u32[]{:S(2)}) async-start(bf16[128,2,4096]{2,1,0:T(2,128)(2,1)} %reshape.52), calls=%async_computation.1 | async-start | bytes 4194304 | tf_op jit(solution)/shard_map/all_to_all | solution.py:35
  41.1 0.5 broadcast.47
  41.6 0.8 reduce.6
  42.4 0.1 eq.44
  42.5 32.1 %all-to-all-done.1 = bf16[128,2,4096]{2,1,0:T(2,128)(2,1)S(1)} async-done(((bf16[128,2,4096]{2,1,0:T(2,128)(2,1)}), bf16[128,2,4096]{2,1,0:T(2,128)(2,1)S(1)}, u32[]{:S(2)}, u32[]{:S(2)}) %all-to-all-start.1) | async-done | bytes 2097184 | tf_op jit(solution)/shard_map/all_to_all | solution.py:35
  74.6 2.2 reshape.53
  76.8 0.0 copy-start.1
  76.8 3.2 %fusion.5 = f32[256]{0:T(256)S(1)} fusion(bf16[256,4096]{1,0:T(8,128)(2,1)} %reshape.53, s32[256]{0:T(256)S(1)} %eq.44, pred[256]{0:T(512)(128)(4,1)S(1)} %broadcast_compare_fusion), kind=kOutput, calls=%fused_computation.15 | convolution fusion | flops 537263872 | bytes 2099456 | tf_op jit(solution)/shard_map/dot_general | solution.py:16
  80.1 0.8 all_to_all.18
  80.8 6.2 %all-to-all-start.2 = ((f32[128,1,2]{2,1,0:T(1,128)}), f32[128,1,2]{2,1,0:T(1,128)S(1)}, u32[]{:S(2)}, u32[]{:S(2)}) async-start(f32[128,1,2]{2,1,0:T(1,128)} %bitcast.1), calls=%async_computation.2 | async-start | bytes 131072 | tf_op jit(solution)/shard_map/all_to_all | solution.py:60
  87.1 9.6 %all-to-all-done.2 = f32[128,1,2]{2,1,0:T(1,128)S(1)} async-done(((f32[128,1,2]{2,1,0:T(1,128)}), f32[128,1,2]{2,1,0:T(1,128)S(1)}, u32[]{:S(2)}, u32[]{:S(2)}) %all-to-all-start.2) | async-done | bytes 1056 | tf_op jit(solution)/shard_map/all_to_all | solution.py:60
  96.7 0.5 broadcast.48
  97.2 0.8 reduce.7
  98.0 0.1 reshape.54
  98.2 1.8 gather_fusion
  99.9 134.5 %all-gather.2.cloned.1.call-done = bf16[4096,4096]{1,0:T(8,128)(2,1)} async-done(((bf16[256,4096]{1,0:T(8,128)(2,1)}), bf16[4096,4096]{1,0:T(8,128)(2,1)}) %all-gather.2.cloned.1.call-update) | async-done | bytes 33554448 | tf_op jit(solution)/shard_map/all_gather | solution.py:73
  234.4 0.0 copy-done.1
  234.4 14.7 %fusion.4 = f32[256]{0:T(256)S(1)} fusion(bf16[256,4096]{1,0:T(8,128)(2,1)S(1)} %copy-done.1, bf16[4096,4096]{1,0:T(8,128)(2,1)} %all-gather.2.cloned.1.call-done, s32[256]{0:T(256)S(1)} %iota_add_fusion), kind=kOutput, calls=%fused_computation.13 | convolution fusion | flops 8593080320 | bytes 35653632 | tf_op jit(solution)/shard_map/dot_general | solution.py:16
  249.2 0.6 broadcast_maximum_fusion
  (7 shorter events, 0.1 us)
Async XLA Ops:
  7.2 2.3 copy-start
  7.2 227.3 %all-gather.2.cloned.1.call-start = ((), (), s32[]{:S(2)}) async-start(), calls=%async_computation.3 | async-start | bytes 35651584 | tf_op jit(solution)/shard_map/all_gather | solution.py:73
  11.4 0.7 copy-start.3
  11.4 14.1 %copy-start.2 = (bf16[128,4096]{1,0:T(8,128)(2,1)S(1)}, bf16[128,4096]{1,0:T(8,128)(2,1)}, u32[]{:S(2)}) copy-start(bf16[128,4096]{1,0:T(8,128)(2,1)} %param.3) | copy-start | bytes 3145732
  14.0 21.1 %all-to-all-start = ((s32[128,1,2]{2,1,0:T(1,128)}), s32[128,1,2]{2,1,0:T(1,128)S(1)}, u32[]{:S(2)}, u32[]{:S(2)}) async-start(s32[128,1,2]{2,1,0:T(1,128)} %bitcast), calls=%async_computation | async-start | bytes 131072 | tf_op jit(solution)/shard_map/all_to_all | solution.py:42
  35.1 39.5 %all-to-all-start.1 = ((bf16[128,2,4096]{2,1,0:T(2,128)(2,1)}), bf16[128,2,4096]{2,1,0:T(2,128)(2,1)S(1)}, u32[]{:S(2)}, u32[]{:S(2)}) async-start(bf16[128,2,4096]{2,1,0:T(2,128)(2,1)} %reshape.52), calls=%async_computation.1 | async-start | bytes 4194304 | tf_op jit(solution)/shard_map/all_to_all | solution.py:35
  76.8 157.6 %copy-start.1 = (bf16[256,4096]{1,0:T(8,128)(2,1)S(1)}, bf16[256,4096]{1,0:T(8,128)(2,1)}, u32[]{:S(2)}) copy-start(bf16[256,4096]{1,0:T(8,128)(2,1)} %fusion.1) | copy-start | bytes 6291460
  80.8 15.9 %all-to-all-start.2 = ((f32[128,1,2]{2,1,0:T(1,128)}), f32[128,1,2]{2,1,0:T(1,128)S(1)}, u32[]{:S(2)}, u32[]{:S(2)}) async-start(f32[128,1,2]{2,1,0:T(1,128)} %bitcast.1), calls=%async_computation.2 | async-start | bytes 131072 | tf_op jit(solution)/shard_map/all_to_all | solution.py:60
Sparse Core Ops, SparseCore 0:
  11.5 222.8 all-gather.1
where the time goes:
time: 257 us
  waiting for transfers between devices  180 us (70%)
  starting transfers between devices  23.7 us (9%)
  matrix products  18 us (7%)
  between operations  14.2 us (6%)
  local copies, waits for them, and re-layouts  11.1 us (4%)
  other arithmetic  9.63 us (4%)
    all_gather x1, waiting for transfers between devices, body(): piece = lax.all_gather(big_units, 'blk', axis=0, tiled=True)  135 us
    all_to_all x1, waiting for transfers between devices, body(): lax.all_to_all(outgoing.reshape(devices, capacity, width), ('blk', 'owner...  32.1 us
    dot_general x2, matrix products, inner_block(): lax.dot_general(left_rows, right_rows, (((1,), (1,)), ((), ())), preferre...  18 us
    all_to_all x1, starting transfers between devices, body(): lax.all_to_all(out_labels.reshape(devices, capacity), ('blk', 'owner'), s...  11.5 us
    all_to_all x1, waiting for transfers between devices, body(): lax.all_to_all(owner_best.reshape(devices, capacity), ('blk', 'owner'), s...  9.59 us
    all_to_all x1, starting transfers between devices, body(): lax.all_to_all(owner_best.reshape(devices, capacity), ('blk', 'owner'), s...  6.25 us
    all_to_all x1, starting transfers between devices, body(): lax.all_to_all(outgoing.reshape(devices, capacity, width), ('blk', 'owner...  5.93 us
  transfers between devices with their start and end apart: 4, of which 4 were waited for; matrix products, arithmetic and copies ran while one was open for 7% of the time, Pallas kernels for 0%

commit v1 on v0

v1 whole, which is shorter than its diff:
```python
import functools

import jax
import jax.numpy as jnp
from jax import lax
from jax.experimental import pallas as pl
from jax.experimental.pallas import tpu as pltpu
from jax.sharding import PartitionSpec as P

MESH = pl.DeviceIdType.MESH
F32 = jnp.float32
BF16 = jnp.bfloat16
CPO = 16
LANES = 128
CHUNK = 32
NC = 8
KC = 1024

HOMES = ((0, 0), (0, -1), (0, -2), (2, -2), (-1, 0), (1, 0), (1, 1), (1, 2))
E0, E1, E2, E3, O1, O2, O3, O4 = range(8)
EARLY_PAIRS = ((E1, E0), (O1, E0), (O2, E0), (O2, E1), (O1, E1), (O2, O1), (O3, O1), (O3, O2))
SMALL_HOPS = [(dy, dz) for dy in range(4) for dz in range(4) if (dy, dz) != (0, 0)]
NEAR_FIRST = (
    (1, 0), (0, 1), (3, 0), (0, 3), (1, 1), (3, 3), (1, 3), (3, 1),
    (2, 2), (2, 0), (0, 2), (2, 1), (1, 2), (2, 3), (3, 2),
)
X_HOPS = ((0, 1), (1, 0), (3, 1), (1, 1), (3, 0), (2, 0), (2, 1))


def pick(index, table):
    value = jnp.int32(table[0])
    for place, entry in enumerate(table[1:], 1):
        value = jnp.where(index == place, jnp.int32(entry), value)
    return value


def nt_dot(a, b):
    return lax.dot_general(a, b, (((1,), (1,)), ((), ())), preferred_element_type=F32)


def unit(values):
    values = values.astype(F32)
    inverse = lax.rsqrt(jnp.sum(values * values, axis=-1, keepdims=True) + 1e-06)
    return (values * inverse).astype(BF16)


def fold(values):
    rows, cols = values.shape
    return jnp.max(values.reshape(rows // 8, 8, cols), axis=0)


def iota(shape, dim):
    return lax.broadcasted_iota(jnp.int32, shape, dim)


def kernel(
    small_ref, cluster_ref, big_ref, small_out, big_out,
    hold, units, sbuf, rbuf, qbuf, tbuf, acc, rowacc, colacc, vsend, vbuf, wsend, wbuf, retsend, ret,
    big_ssem, big_rsem, yz_ssem, yz_rsem, x_ssem, x_rsem, v_ssem, v_rsem, w_ssem, w_rsem, ret_ssem, ret_rsem,
):
    width = small_ref.shape[1]
    wide = width + LANES
    rows = small_ref.shape[0]
    slots = 2 * rows
    b = lax.axis_index("blk")
    o = lax.axis_index("owner")
    z, y = b // 4, b % 4
    x, core = o // 2, o % 2
    sign = 1 - 2 * core
    hub = (y + core) % 2 == 0

    def blk_at(dy, dz):
        return (z + dz + 4) % 4 * 4 + (y + dy + 4) % 4

    def turned(dy, dz):
        return {"blk": blk_at(sign * dy, dz), "owner": o}

    def row_at(dx, dc):
        return (x + dx) % 4 * 2 + (core + dc) % 2

    barrier = pltpu.get_barrier_semaphore()
    for dy, dz in SMALL_HOPS:
        pl.semaphore_signal(barrier, inc=1, device_id={"blk": blk_at(dy, dz), "owner": o}, device_id_type=MESH)
    for dx, dc in X_HOPS:
        pl.semaphore_signal(barrier, inc=1, device_id={"blk": b, "owner": row_at(dx, dc)}, device_id_type=MESH)

    cluster_lanes = jnp.broadcast_to(cluster_ref[...], (rows, rows))
    cluster_rows = jnp.transpose(cluster_lanes.astype(F32)).astype(jnp.int32)
    owner_lanes, owner_rows = cluster_lanes // CPO, cluster_rows // CPO
    earlier = (owner_lanes == owner_rows) & (iota((rows, rows), 0) < iota((rows, rows), 1))
    rank = jnp.sum(jnp.where(earlier, 1.0, 0.0), axis=0, keepdims=True).astype(jnp.int32)
    owner_of_doc = cluster_ref[...] // CPO
    slot_of_doc = owner_of_doc * 2 + rank
    place = jnp.where(iota((slots, rows), 0) == slot_of_doc, 1.0, 0.0).astype(BF16)
    label = jnp.where(iota((rows, LANES), 1) == cluster_rows % CPO, 1.0, 0.0).astype(BF16)

    @pl.loop(0, rows // 16)
    def _(step):
        at = pl.ds(pl.multiple_of(step * 16, 16), 16)
        units[at, :] = unit(small_ref[at, :])

    @pl.loop(0, width // 512)
    def _(step):
        at = pl.ds(pl.multiple_of(step * 512, 512), 512)
        sbuf[:, at] = jnp.dot(place, units[:, at], preferred_element_type=F32).astype(BF16)

    sbuf[:, pl.ds(width, LANES)] = jnp.dot(place, label, preferred_element_type=F32).astype(BF16)

    pl.semaphore_wait(barrier, len(SMALL_HOPS) + len(X_HOPS))

    def yz_copy(n):
        dy, dz = NEAR_FIRST[n]
        to = blk_at(dy, dz)
        return pltpu.make_async_remote_copy(
            src_ref=sbuf.at[pl.ds(pl.multiple_of(to * 16, 16), 16)],
            dst_ref=rbuf.at[pl.ds(pl.multiple_of(b * 16, 16), 16)],
            send_sem=yz_ssem.at[n],
            recv_sem=yz_rsem.at[n],
            device_id={"blk": to, "owner": o},
            device_id_type=MESH,
        )

    for n in range(15):
        yz_copy(n).start()
    mine = pl.ds(pl.multiple_of(b * 16, 16), 16)
    rbuf[mine, :] = sbuf[mine, :]

    def big_copy(lane, c, slot, to_slot, to):
        at = pl.ds(pl.multiple_of(c * CHUNK, CHUNK), CHUNK)
        return pltpu.make_async_remote_copy(
            src_ref=hold.at[slot, at],
            dst_ref=hold.at[to_slot, at],
            send_sem=big_ssem.at[lane, c],
            recv_sem=big_rsem.at[to_slot, c],
            device_id=turned(*to),
            device_id_type=MESH,
        )

    def own_right(c):
        return big_copy(0, c, E0, E1, (0, 1))

    def e1_right(c):
        return big_copy(1, c, E1, E2, (0, 1))

    def e2_down(c):
        return big_copy(2, c, E2, 1, (-1, 0))

    def o2_left(c):
        return big_copy(3, c, O2, O3, (0, -1))

    def o3_left(c):
        return big_copy(4, c, O3, O4, (0, -1))

    def own_up(c):
        return big_copy(0, c, 0, O1, (1, 0))

    def own_down(c):
        return big_copy(1, c, 0, O2, (-1, 0))

    def relay_down(c):
        return big_copy(2, c, 1, E3, (-1, 0))

    def arrived(slot, c):
        big_copy(0, c, slot, slot, (0, 1)).wait_recv()

    @pl.loop(0, NC)
    def _(c):
        for part in range(CHUNK // 16):
            at = pl.ds(pl.multiple_of(c * CHUNK + part * 16, 16), 16)
            hold[0, at, :] = unit(big_ref[at, :])

        @pl.when(hub)
        def _():
            own_right(c).start()

        @pl.when(jnp.logical_not(hub))
        def _():
            own_down(c).start()
            own_up(c).start()

    rowacc[...] = jnp.full(rowacc.shape, -1.0, F32)
    colacc[...] = jnp.full(colacc.shape, -1.0, F32)

    def product(m, left, right):
        acc[pl.ds(0, m), :] = nt_dot(left(0), right(0))

        @pl.loop(1, width // KC)
        def _(k):
            acc[pl.ds(0, m), :] += nt_dot(left(k), right(k))

    def features(k):
        return pl.ds(pl.multiple_of(k * KC, KC), KC)

    def pair(i, r, m, j):
        at = pl.ds(r, m)
        product(m, lambda k: hold[i, at, features(k)], lambda k: hold[j, :, features(k)])
        gram = acc[pl.ds(0, m), :]
        half = gram.shape[1] // 2
        rowacc[i, at, :] = jnp.maximum(rowacc[i, at, :], jnp.maximum(gram[:, :half], gram[:, half:]))
        colacc[j] = jnp.maximum(colacc[j], fold(gram))

    def own_pairs():
        product(hold.shape[1], lambda k: hold[0, :, features(k)], lambda k: hold[0, :, features(k)])
        gram = acc[...]
        gram = jnp.where(iota(gram.shape, 0) == iota(gram.shape, 1), -1.0, gram)
        colacc[0] = jnp.maximum(colacc[0], fold(gram))

    def some_pairs(table, r, m):
        @pl.loop(0, len(table))
        def _(p):
            pair(pick(p, [t[0] for t in table]), r, m, pick(p, [t[1] for t in table]))

    def on(role, body):
        pl.when(hub if role else jnp.logical_not(hub))(body)

    def x_copy(n):
        dx, dc = X_HOPS[n]
        to = row_at(dx, dc)
        return pltpu.make_async_remote_copy(
            src_ref=qbuf.at[pl.ds(pl.multiple_of(to * 32, 32), 32)],
            dst_ref=tbuf.at[pl.ds(pl.multiple_of(o * 32, 32), 32)],
            send_sem=x_ssem.at[n],
            recv_sem=x_rsem.at[n],
            device_id={"blk": b, "owner": to},
            device_id_type=MESH,
        )

    def regroup():
        for n in range(15):
            yz_copy(n).wait_recv()
        to_row = iota((slots, slots), 0)
        source = to_row % 32 // 2 * 16 + to_row // 32 * 2 + to_row % 2
        move = jnp.where(iota((slots, slots), 1) == source, 1.0, 0.0).astype(BF16)

        @pl.loop(0, width // 512)
        def _(step):
            at = pl.ds(pl.multiple_of(step * 512, 512), 512)
            qbuf[:, at] = jnp.dot(move, rbuf[:, at], preferred_element_type=F32).astype(BF16)

        tail = pl.ds(width, LANES)
        qbuf[:, tail] = jnp.dot(move, rbuf[:, tail], preferred_element_type=F32).astype(BF16)
        for n in range(7):
            x_copy(n).start()
        here = pl.ds(pl.multiple_of(o * 32, 32), 32)
        tbuf[here, :] = qbuf[here, :]

    def v_copy(n):
        to = row_at(*X_HOPS[n])
        return pltpu.make_async_remote_copy(
            src_ref=vsend, dst_ref=vbuf.at[o], send_sem=v_ssem.at[n], recv_sem=v_rsem.at[n],
            device_id={"blk": b, "owner": to}, device_id_type=MESH,
        )

    def w_copy(n):
        to = blk_at(*NEAR_FIRST[n])
        return pltpu.make_async_remote_copy(
            src_ref=wsend, dst_ref=wbuf.at[b], send_sem=w_ssem.at[n], recv_sem=w_rsem.at[n],
            device_id={"blk": to, "owner": o}, device_id_type=MESH,
        )

    def owner_maxima():
        for n in range(7):
            x_copy(n).wait_recv()
        product(slots, lambda k: tbuf[:, features(k)], lambda k: tbuf[:, features(k)])
        labels = tbuf[:, pl.ds(width, LANES)]
        same = nt_dot(labels, labels) > 0.5
        same = same & (iota((slots, slots), 0) != iota((slots, slots), 1))
        best = jnp.max(jnp.where(same, acc[...], -1.0), axis=0, keepdims=True)
        vsend[...] = jnp.broadcast_to(best, vsend.shape)
        for n in range(7):
            v_copy(n).start()
        vbuf[o] = vsend[...]

    def pass_back():
        for n in range(7):
            v_copy(n).wait_recv()
        packed = vbuf[0]
        for other in range(1, 8):
            packed = jnp.where(iota(packed.shape, 0) == other, vbuf[other], packed)
        packed = pltpu.roll(packed, (8 - o) * 32 % slots, 1)
        wsend[...] = packed[:, :LANES]
        for n in range(15):
            w_copy(n).start()
        wbuf[b] = wsend[...]

    def small_result():
        for n in range(15):
            w_copy(n).wait_recv()
        table = wbuf[...].reshape(16 * 8, LANES)
        chosen = jnp.where(iota((16 * 8, rows), 0) == owner_of_doc, 1.0, 0.0)
        found = lax.dot_general(
            table, chosen, (((0,), (0,)), ((), ())), precision=lax.Precision.HIGHEST, preferred_element_type=F32
        )
        found = jnp.where(iota(found.shape, 0) == 2 * b + rank, found, 0.0)
        small_out[...] = jnp.sum(found, axis=0, keepdims=True)

    def first_steps(start, stop):
        def body():
            @pl.loop(start, stop)
            def _(c):
                arrived(O2, c)
                o2_left(c).start()

                @pl.when(c >= 5)
                def _():
                    arrived(E1, c - 5)
                    e1_right(c - 5).start()
                    arrived(O3, c - 5)
                    o3_left(c - 5).start()

        return body

    on(True, first_steps(0, 1))
    regroup()
    on(True, first_steps(1, NC))

    def rest_of_first():
        @pl.loop(3, NC)
        def _(c):
            arrived(E1, c)
            e1_right(c).start()
            arrived(O3, c)
            o3_left(c).start()

        @pl.loop(0, NC)
        def _(c):
            arrived(O1, c)

    on(True, rest_of_first)

    def second_steps(start, stop):
        def body():
            @pl.loop(start, stop)
            def _(c):
                arrived(E2, c)
                e2_down(c).start()
                pair(pick(c, [t[0] for t in EARLY_PAIRS]), 0, 256, pick(c, [t[1] for t in EARLY_PAIRS]))

        return body

    def relay_steps(start, stop):
        def body():
            @pl.loop(start, stop)
            def _(c):
                arrived(1, c)
                relay_down(c).start()

        return body

    on(False, relay_steps(0, 4))
    on(True, second_steps(0, 4))
    own_pairs()
    owner_maxima()
    on(False, relay_steps(4, 6))
    on(True, second_steps(4, 6))
    pass_back()
    on(False, relay_steps(6, NC))
    on(True, second_steps(6, NC))

    def half_pairs(start):
        @pl.loop(0, 4)
        def _(c):
            arrived(O4, c + start // CHUNK)

        some_pairs(((E2, E0), (E2, O1), (E2, O2), (E2, O3), (O4, O1), (O4, O2)), start, 128)

    def late_pairs():
        half_pairs(0)
        half_pairs(128)

    on(True, late_pairs)
    small_result()

    def finish(slot):
        whole = jnp.maximum(fold(jnp.transpose(rowacc[slot])), colacc[slot])
        return jnp.broadcast_to(jnp.max(whole, axis=0, keepdims=True), whole.shape)

    def home_copy(slot):
        return pltpu.make_async_remote_copy(
            src_ref=retsend.at[slot], dst_ref=ret.at[slot], send_sem=ret_ssem.at[slot], recv_sem=ret_rsem.at[slot],
            device_id=turned(*HOMES[slot]), device_id_type=MESH,
        )

    def send_home(slots_done):
        for slot in slots_done:
            retsend[slot] = finish(slot)
            home_copy(slot).start()

    def last_pairs():
        send_home((O1, O2, O4))

        @pl.loop(0, 4)
        def _(c):
            arrived(E3, c)

        last = ((E3, E0), (E3, E1), (E3, O3), (E3, E2))
        some_pairs(last, 0, 128)

        @pl.loop(4, NC)
        def _(c):
            arrived(E3, c)

        some_pairs(last, 128, 128)
        send_home((E3, E2, E1, O3))
        retsend[0] = finish(0)
        for slot in (E1, E2, E3):
            home_copy(slot).wait_recv()
            retsend[0] = jnp.maximum(retsend[0], ret[slot])
        big_out[...] = retsend[0][0:1]

        for slot in range(1, 8):
            home_copy(slot).wait_send()

        @pl.loop(0, NC)
        def _(c):
            own_right(c).wait_send()
            e1_right(c).wait_send()
            e2_down(c).wait_send()
            o2_left(c).wait_send()
            o3_left(c).wait_send()

    def last_relay():
        retsend[0] = finish(0)
        for slot in (O1, O2, O3, O4):
            home_copy(slot).wait_recv()
            retsend[0] = jnp.maximum(retsend[0], ret[slot])
        big_out[...] = retsend[0][0:1]

        @pl.loop(0, NC)
        def _(c):
            own_up(c).wait_send()
            own_down(c).wait_send()
            relay_down(c).wait_send()

    on(True, last_pairs)
    on(False, last_relay)
    for n in range(15):
        yz_copy(n).wait_send()
        w_copy(n).wait_send()
    for n in range(7):
        x_copy(n).wait_send()
        v_copy(n).wait_send()


def body(small_emb, cluster_of, big_emb):
    rows, width = small_emb.shape
    count = big_emb.shape[0]
    wide = width + LANES
    dma = pltpu.SemaphoreType.DMA
    small_max, big_max = pl.pallas_call(
        kernel,
        out_shape=(jax.ShapeDtypeStruct((1, rows), F32), jax.ShapeDtypeStruct((1, count), F32)),
        in_specs=[pl.BlockSpec(memory_space=pltpu.VMEM)] * 3,
        out_specs=[pl.BlockSpec(memory_space=pltpu.VMEM)] * 2,
        scratch_shapes=[
            pltpu.VMEM((8, count, width), BF16),
            pltpu.VMEM((rows, width), BF16),
            pltpu.VMEM((2 * rows, wide), BF16),
            pltpu.VMEM((2 * rows, wide), BF16),
            pltpu.VMEM((2 * rows, wide), BF16),
            pltpu.VMEM((2 * rows, wide), BF16),
            pltpu.VMEM((count, count), F32),
            pltpu.VMEM((8, count, count // 2), F32),
            pltpu.VMEM((8, 8, count), F32),
            pltpu.VMEM((8, 2 * rows), F32),
            pltpu.VMEM((8, 8, 2 * rows), F32),
            pltpu.VMEM((8, LANES), F32),
            pltpu.VMEM((16, 8, LANES), F32),
            pltpu.VMEM((8, 8, count), F32),
            pltpu.VMEM((8, 8, count), F32),
            dma((5, NC)), dma((8, NC)), dma((15,)), dma((15,)), dma((7,)), dma((7,)),
            dma((7,)), dma((7,)), dma((15,)), dma((15,)), dma((8,)), dma((8,)),
        ],
        compiler_params=pltpu.CompilerParams(
            collective_id=0, has_side_effects=True, vmem_limit_bytes=56 * 2**20
        ),
    )(small_emb, cluster_of.reshape(1, rows), big_emb)
    return small_max.reshape(rows), big_max.reshape(count)


def solution(mesh):
    return jax.shard_map(
        body,
        mesh=mesh,
        in_specs=(P(("blk", "owner"), None), P(("blk", "owner")), P(("blk", "owner"), None)),
        out_specs=(P(("blk", "owner")), P(("blk", "owner"))),
        check_vma=False,
    )
```

time: 257 us -> 130 us (0.51)
  the two profiles are of different devices: /device:TPU:1 before, /device:TPU:9 now
where the time goes in v1:
time: 130 us
  Pallas kernels  127 us (98%)
  local copies, waits for them, and re-layouts  2.36 us (2%)
    pallas_call x1, Pallas kernels, body(): pl.pallas_call(kernel, out_shape=(jax.ShapeDtypeStruct((1, rows), F32), j...  127 us

profile of v1, /device:TPU:9, one launch (start us, length us, event | category | flops | bytes accessed | tf_op | source)
XLA Modules:
  0.0 129.7 jit_solution(2547070596849812522)
XLA Ops:
  0.6 126.7 %shard_map.50 = (f32[1,128]{1,0:T(1,128)}, f32[1,256]{1,0:T(1,128)}) custom-call(bf16[128,4096]{1,0:T(8,128)(2,1)} %small_ref.1, s32[1,128]{1,0:T(1,128)} %bitcast.4, bf16[256,4096]{1,0:T(8,128)(2,1)} %big_ref.1), custom_call_target="tpu_custom_call" | custom-call | tf_op jit(solution)/shard_map/pallas_call | solution.py:450
  127.4 1.1 copy.7
  128.5 1.2 copy.8
